TPU v7x, 32 devices: a whole 2x2x4 slice. The times are simulated.
32 devices in a mesh: tm: 8 (over z, core), space: 4 (over y, x).
Axes of the slice: x: 2, y: 2, z: 4, core: 2. Of those that a mesh axis runs over, the one named last changes fastest.
Arguments:
- features: bfloat16 [32, 64, 128, 128], P('tm', 'space'), may hold values from -6 to 6
- kernel_first: bfloat16 [3, 3, 3, 128, 128], replicated, may hold values from -0.109375 to 0.109375
- bias_first: float32 [128], replicated, may hold values from -3 to 3
- kernel_down: bfloat16 [3, 3, 128, 256], replicated, may hold values from -0.1875 to 0.1875
- bias_down: float32 [256], replicated, may hold values from -3 to 3
- kernel_second: bfloat16 [3, 3, 3, 256, 256], replicated, may hold values from -0.078125 to 0.078125
- bias_second: float32 [256], replicated, may hold values from -3 to 3
Outputs:
- latent: bfloat16 [32, 32, 64, 256], P('tm', 'space')
All inputs are finite; a program needn't handle non-finite values.
Results may differ from a plain program's by a relative error of at most 0.0095.
Values may be sent and summed in bfloat16 or wider, within the bound.
A program may use at most 64 MiB of HBM per device.

v0:
```python
import functools

import jax
import jax.numpy as jnp
from jax import lax
from jax.experimental import pallas as pl
from jax.experimental.pallas import tpu as pltpu
from jax.sharding import PartitionSpec as P

MESH = pl.DeviceIdType.MESH
BF = jnp.bfloat16
F32 = jnp.float32


def silu(v):
    h = 0.5 * v
    return h + h * jnp.tanh(h)


def before(x, width):
    p = lax.broadcasted_iota(jnp.int32, x.shape, 0) % width
    return jnp.where(p == 0, 0.0, pltpu.roll(x, 1, 0))


def after(x, width):
    p = lax.broadcasted_iota(jnp.int32, x.shape, 0) % width
    return jnp.where(p == width - 1, 0.0, pltpu.roll(x, x.shape[0] - 1, 0))


def kernel(
    nt, ns, x, b1, bd, b2, k1, kd, k2, out,
    hx, hr, lines, act, feat, w1, wd, w2, fo, red, mid, res,
    send, recv, wsem, osem,
):
    t, s = lax.axis_index("tm"), lax.axis_index("space")
    frames, rows, cols, c0 = x.shape
    pairs = cols // 2
    half = rows // 2
    c1 = res.shape[-1]

    def there(dt, ds):
        ok = None
        for pos, step, count in ((t, dt, nt), (s, ds, ns)):
            if step:
                this = pos < count - 1 if step > 0 else pos > 0
                ok = this if ok is None else jnp.logical_and(ok, this)
        return ok

    around = [(dt, ds) for dt in (-1, 0, 1) for ds in (-1, 0, 1) if dt or ds]

    def place(dt, ds):
        return (lax.rem(t + dt + nt, nt), lax.rem(s + ds + ns, ns))

    weights = [
        pltpu.make_async_copy(src, dst, wsem.at[n])
        for n, (src, dst) in enumerate(
            [
                (k1.at[:, :, 1], w1.at[:, :, 0:c0, 0:c0]),
                (k1.at[:, :, 0], w1.at[:, :, 0:c0, c0:2 * c0]),
                (k1.at[:, :, 2], w1.at[:, :, 0:c0, 3 * c0:4 * c0]),
                (k1.at[:, :, 2], w1.at[:, :, c0:2 * c0, 0:c0]),
                (k1.at[:, :, 1], w1.at[:, :, c0:2 * c0, c0:2 * c0]),
                (k1.at[:, :, 0], w1.at[:, :, c0:2 * c0, 2 * c0:3 * c0]),
                (kd.at[:, 1], wd.at[:, 0:c0, 0:c1]),
                (kd.at[:, 2], wd.at[:, c0:2 * c0, 0:c1]),
                (kd.at[:, 0], wd.at[:, c0:2 * c0, c1:2 * c1]),
                (k2.at[:, :, 0], w2.at[:, :, :, 0:c1]),
                (k2.at[:, :, 1], w2.at[:, :, :, c1:2 * c1]),
                (k2.at[:, :, 2], w2.at[:, :, :, 2 * c1:3 * c1]),
            ]
        )
    ]
    for copy in weights:
        copy.start()

    barrier = pltpu.get_barrier_semaphore()
    for dt, ds in around:
        @pl.when(there(dt, ds))
        def _():
            pl.semaphore_signal(barrier, inc=1, device_id=place(dt, ds), device_id_type=MESH)
    near_t = jnp.where(t > 0, 1, 0) + jnp.where(t < nt - 1, 1, 0) + 1
    near_s = jnp.where(s > 0, 1, 0) + jnp.where(s < ns - 1, 1, 0) + 1
    pl.semaphore_wait(barrier, near_t * near_s - 1)

    plan = {}

    def add(name, src, dst, dt, ds):
        plan[name] = (src, dst, len(plan), dt, ds)

    last, prev = frames - 1, frames - 2
    add("up", x.at[:, 0], hr.at[1], 0, -1)
    add("down", x.at[:, rows - 1], hr.at[0], 0, 1)
    add("t1", x.at[last], hx.at[1, 1:rows + 1], 1, 0)
    add("tu", x.at[prev:frames, 0], hx.at[:, rows + 1], 1, -1)
    add("td", x.at[prev:frames, rows - 1], hx.at[:, 0], 1, 1)
    add("t0", x.at[prev], hx.at[0, 1:rows + 1], 1, 0)
    for f in range(frames):
        add(f"fo{f}", fo.at[f, rows], fo.at[f, 0], 0, 1)
        add(f"mu{f}", mid.at[f + 2, 1], mid.at[f + 2, half + 1], 0, -1)
        add(f"md{f}", mid.at[f + 2, half], mid.at[f + 2, 0], 0, 1)
        if f >= prev:
            g = f - prev
            add(f"mt{f}", mid.at[f + 2, 1:half + 1], mid.at[g, 1:half + 1], 1, 0)
            add(f"ma{f}", mid.at[f + 2, 1], mid.at[g, half + 1], 1, -1)
            add(f"mb{f}", mid.at[f + 2, half], mid.at[g, 0], 1, 1)

    def remote(name):
        src, dst, n, dt, ds = plan[name]
        return pltpu.make_async_remote_copy(
            src_ref=src, dst_ref=dst, send_sem=send.at[n], recv_sem=recv.at[n],
            device_id=place(dt, ds), device_id_type=MESH,
        )

    def start(*names):
        for name in names:
            @pl.when(there(*plan[name][3:]))
            def _():
                remote(name).start()

    def arrived(*names):
        for name in names:
            _, _, _, dt, ds = plan[name]
            @pl.when(there(-dt, -ds))
            def _():
                remote(name).wait_recv()

    start("up", "down", "t1", "tu", "td", "t0")

    @pl.when(t == 0)
    def _():
        hx[...] = jnp.zeros_like(hx)
        mid[0:2] = jnp.zeros((2,) + mid.shape[1:], BF)

    @pl.when(s == 0)
    def _():
        hr[0] = jnp.zeros(hr.shape[1:], BF)
        fo[:, 0] = jnp.zeros((frames, pairs, 2 * c0), BF)
        mid[2:, 0] = jnp.zeros((frames, pairs, c1), BF)

    @pl.when(s == ns - 1)
    def _():
        hr[1] = jnp.zeros(hr.shape[1:], BF)
        mid[2:, half + 1] = jnp.zeros((frames, pairs, c1), BF)

    @pl.when(jnp.logical_and(t > 0, s == 0))
    def _():
        hx[:, 0] = jnp.zeros((2, cols, c0), BF)
        mid[0:2, 0] = jnp.zeros((2, pairs, c1), BF)

    @pl.when(jnp.logical_and(t > 0, s == ns - 1))
    def _():
        hx[:, rows + 1] = jnp.zeros((2, cols, c0), BF)
        mid[0:2, half + 1] = jnp.zeros((2, pairs, c1), BF)

    w1[:, :, 0:c0, 2 * c0:3 * c0] = jnp.zeros((3, 3, c0, c0), BF)
    w1[:, :, c0:2 * c0, 3 * c0:4 * c0] = jnp.zeros((3, 3, c0, c0), BF)
    wd[:, 0:c0, c1:2 * c1] = jnp.zeros((3, c0, c1), BF)

    def paired(value):
        count = value.shape[0]
        lines[0:count * cols] = value.reshape(count * cols, c0).astype(F32)
        even = lines[pl.ds(0, count * pairs, stride=2), :]
        odd = lines[pl.ds(1, count * pairs, stride=2), :]
        both = jnp.concatenate([even, odd], axis=1)
        return both.reshape(count, pairs, 2 * c0)

    step = 4

    def own(n, carry):
        f, r = n // (rows // step), (n % (rows // step)) * step
        both = paired(x[f, pl.ds(r, step)])
        feat[f, pl.ds(r, step)] = both.astype(BF)
        act[f + 2, pl.ds(r + 1, step)] = silu(both).astype(BF)
        return carry

    lax.fori_loop(0, frames * rows // step, own, 0)
    arrived("up", "down")
    for side, row in ((0, 0), (1, rows + 1)):
        act[2:, row] = silu(paired(hr[side])).astype(BF)

    for copy in weights[:6]:
        copy.wait()

    block = 8

    def conv_first(f):
        def body(n, carry):
            r = n * block
            left = jnp.concatenate(
                [
                    act[f + i, pl.ds(r + j, block)].reshape(block * pairs, 2 * c0)
                    for i in range(3) for j in range(3)
                ],
                axis=1,
            )
            total = jnp.dot(left, w1[...].reshape(9 * 2 * c0, 4 * c0), preferred_element_type=F32)
            bias = b1[...]
            base = feat[f, pl.ds(r, block)].reshape(block * pairs, 2 * c0).astype(F32)
            even = base[:, :c0] + bias + total[:, :c0] + before(total[:, 2 * c0:3 * c0], pairs)
            odd = base[:, c0:] + bias + total[:, c0:2 * c0] + after(total[:, 3 * c0:], pairs)
            both = jnp.concatenate([even, odd], axis=1).astype(BF)
            fo[f, pl.ds(r + 1, block)] = both.reshape(block, pairs, 2 * c0)
            return carry

        lax.fori_loop(0, rows // block, body, 0)
        start(f"fo{f}")

    def downsample(f):
        arrived(f"fo{f}")
        left = jnp.concatenate(
            [
                jnp.concatenate([fo[f, 2 * r + j][None] for r in range(half)], axis=0).reshape(half * pairs, 2 * c0)
                for j in range(3)
            ],
            axis=1,
        )
        total = jnp.dot(left, wd[...].reshape(3 * 2 * c0, 2 * c1), preferred_element_type=F32)
        value = (total[:, :c1] + before(total[:, c1:], pairs) + bd[...]).astype(BF)
        red[f] = value.reshape(half, pairs, c1)
        mid[f + 2, 1:half + 1] = silu(value.astype(F32)).astype(BF).reshape(half, pairs, c1)
        if f >= prev:
            start(f"mt{f}", f"ma{f}", f"mb{f}")
        start(f"mu{f}", f"md{f}")

    def conv_second(f):
        left = jnp.concatenate(
            [
                mid[f + i, j:j + half].reshape(half * pairs, c1)
                for i in range(3) for j in range(3)
            ],
            axis=1,
        )
        total = jnp.dot(left, w2[...].reshape(9 * c1, 3 * c1), preferred_element_type=F32)
        value = red[f].reshape(half * pairs, c1).astype(F32) + b2[...]
        value = value + total[:, c1:2 * c1] + before(total[:, :c1], pairs) + after(total[:, 2 * c1:], pairs)
        res[f] = value.astype(BF).reshape(half, pairs, c1)
        pltpu.make_async_copy(res.at[f], out.at[f], osem.at[f]).start()

    def halo(g):
        def body(n, carry):
            act[g, pl.ds(n * 3, 3)] = silu(paired(hx[g, pl.ds(n * 3, 3)])).astype(BF)
            return carry

        lax.fori_loop(0, (rows + 2) // 3, body, 0)

    conv_first(3)
    conv_first(2)
    for copy in weights[6:9]:
        copy.wait()
    downsample(3)
    arrived("t1", "tu", "td")
    halo(1)
    conv_first(1)
    downsample(2)
    arrived("t0")
    halo(0)
    conv_first(0)
    downsample(1)
    downsample(0)
    for copy in weights[9:]:
        copy.wait()
    for f in range(frames):
        arrived(f"mu{f}", f"md{f}")
    conv_second(3)
    conv_second(2)
    arrived("mt3", "ma3", "mb3")
    conv_second(1)
    arrived("mt2", "ma2", "mb2")
    conv_second(0)

    for name in plan:
        @pl.when(there(*plan[name][3:]))
        def _():
            remote(name).wait_send()
    for f in range(frames):
        pltpu.make_async_copy(res.at[f], out.at[f], osem.at[f]).wait()


def on_device(nt, ns, x, k1, b1, kd, bd, k2, b2):
    frames, rows, cols, c0 = x.shape
    c1 = kd.shape[-1]
    half, pairs = rows // 2, cols // 2
    vmem = pl.BlockSpec(memory_space=pltpu.VMEM)
    hbm = pl.BlockSpec(memory_space=pl.ANY)
    copies = 6 + 3 * frames + 6
    return pl.pallas_call(
        functools.partial(kernel, nt, ns),
        out_shape=jax.ShapeDtypeStruct((frames, half, pairs, c1), BF),
        in_specs=[vmem] * 4 + [hbm] * 3,
        out_specs=hbm,
        scratch_shapes=[
            pltpu.VMEM((2, rows + 2, cols, c0), BF),
            pltpu.VMEM((2, frames, cols, c0), BF),
            pltpu.VMEM((4 * cols, c0), F32),
            pltpu.VMEM((frames + 2, rows + 2, pairs, 2 * c0), BF),
            pltpu.VMEM((frames, rows, pairs, 2 * c0), BF),
            pltpu.VMEM((3, 3, 2 * c0, 4 * c0), BF),
            pltpu.VMEM((3, 2 * c0, 2 * c1), BF),
            pltpu.VMEM((3, 3, c1, 3 * c1), BF),
            pltpu.VMEM((frames, rows + 1, pairs, 2 * c0), BF),
            pltpu.VMEM((frames, half, pairs, c1), BF),
            pltpu.VMEM((frames + 2, half + 2, pairs, c1), BF),
            pltpu.VMEM((frames, half, pairs, c1), BF),
            pltpu.SemaphoreType.DMA((copies,)),
            pltpu.SemaphoreType.DMA((copies,)),
            pltpu.SemaphoreType.DMA((12,)),
            pltpu.SemaphoreType.DMA((frames,)),
        ],
        compiler_params=pltpu.CompilerParams(
            collective_id=0, has_side_effects=True, vmem_limit_bytes=60 * 1024 * 1024
        ),
        cost_estimate=pl.CostEstimate(flops=16 * 10**9, bytes_accessed=10**7, transcendentals=0),
    )(x, b1[None], bd[None], b2[None], k1, kd, k2)


def solution(mesh):
    in_specs = (P("tm", "space", None, None), P(), P(), P(), P(), P(), P())
    out_specs = P("tm", "space", None, None)
    sizes = mesh.shape["tm"], mesh.shape["space"]
    return jax.shard_map(
        functools.partial(on_device, *sizes), mesh=mesh, in_specs=in_specs, out_specs=out_specs, check_vma=False
    )
```

profile of v0, /device:TPU:20, one launch (start us, length us, event | category | flops | bytes accessed | tf_op | source)
XLA Modules:
  0.0 44.1 jit_solution(17943447367392378964)
XLA Ops:
  0.0 41.8 %shard_map.73 = bf16[4,8,64,256]{3,2,1,0:T(8,128)(2,1)} custom-call(bf16[4,16,128,128]{3,2,1,0:T(8,128)(2,1)} %x.1, f32[1,128]{1,0:T(1,128)} %bitcast.5, f32[1,256]{1,0:T(1,128)} %bitcast.3, f32[1,256]{1,0:T(1,128)} %bitcast.4, bf16[3,3,3,128,128]{4,3,2,1,0:T(8,128)(2,1)} %k1.1, bf16[3,3,128,256]{3,2,1,0:T(8,128)(2,1)} %kd.1, bf16[3,3,3,256,256]{4,3,2,1,0:T(8,128)(2,1)} %k2.1), custom_call_target="tpu_custom_call" | custom-call | flops 16000000000 | bytes 10000000 | tf_op jit(solution)/shard_map/pallas_call | solution.py:286
  41.8 2.3 %copy.9 = bf16[4,8,64,256]{3,2,1,0:T(8,128)(2,1)} copy(bf16[4,8,64,256]{3,2,1,0:T(8,128)(2,1)} %shard_map.73) | data formatting | bytes 2097152
where the time goes:
time: 44.4 us; the launch traced here: 44.1 us
  Pallas kernels  41.8 us (94%)
  local copies, waits for them, and re-layouts  2.3 us (5%)
    pallas_call x1, Pallas kernels, on_device(): pl.pallas_call(functools.partial(kernel, nt, ns), out_shape=jax.ShapeDtyp...  41.8 us
    unnamed x1, local copies, waits for them, and re-layouts  2.3 us

commit v1 on v0

--- a/solution.py
+++ b/solution.py
@@ -17,19 +17,26 @@
     return h + h * jnp.tanh(h)
 
 
+def edge(shape, width, row):
+    at = lax.broadcasted_iota(jnp.int32, (width, shape[1]), 0) == row
+    return jnp.broadcast_to(at[None], (shape[0] // width,) + at.shape).reshape(shape)
+
+
 def before(x, width):
-    p = lax.broadcasted_iota(jnp.int32, x.shape, 0) % width
-    return jnp.where(p == 0, 0.0, pltpu.roll(x, 1, 0))
+    return jnp.where(edge(x.shape, width, 0), 0.0, pltpu.roll(x, 1, 0))
 
 
 def after(x, width):
-    p = lax.broadcasted_iota(jnp.int32, x.shape, 0) % width
-    return jnp.where(p == width - 1, 0.0, pltpu.roll(x, x.shape[0] - 1, 0))
+    return jnp.where(edge(x.shape, width, width - 1), 0.0, pltpu.roll(x, x.shape[0] - 1, 0))
+
+
+def products(d0, d1, d2, d3):
+    return d0 - d2, d1 + d2, d2 - d1, d1 - d3
 
 
 def kernel(
     nt, ns, x, b1, bd, b2, k1, kd, k2, out,
-    hx, hr, lines, act, feat, w1, wd, w2, fo, red, mid, res,
+    hx, hr, lines, act, feat, v1, u1, wd, v2, u2, fo, red, mid, res, sums,
     send, recv, wsem, osem,
 ):
     t, s = lax.axis_index("tm"), lax.axis_index("space")
@@ -51,25 +58,20 @@
     def place(dt, ds):
         return (lax.rem(t + dt + nt, nt), lax.rem(s + ds + ns, ns))
 
-    weights = [
-        pltpu.make_async_copy(src, dst, wsem.at[n])
-        for n, (src, dst) in enumerate(
-            [
-                (k1.at[:, :, 1], w1.at[:, :, 0:c0, 0:c0]),
-                (k1.at[:, :, 0], w1.at[:, :, 0:c0, c0:2 * c0]),
-                (k1.at[:, :, 2], w1.at[:, :, 0:c0, 3 * c0:4 * c0]),
-                (k1.at[:, :, 2], w1.at[:, :, c0:2 * c0, 0:c0]),
-                (k1.at[:, :, 1], w1.at[:, :, c0:2 * c0, c0:2 * c0]),
-                (k1.at[:, :, 0], w1.at[:, :, c0:2 * c0, 2 * c0:3 * c0]),
-                (kd.at[:, 1], wd.at[:, 0:c0, 0:c1]),
-                (kd.at[:, 2], wd.at[:, c0:2 * c0, 0:c1]),
-                (kd.at[:, 0], wd.at[:, c0:2 * c0, c1:2 * c1]),
-                (k2.at[:, :, 0], w2.at[:, :, :, 0:c1]),
-                (k2.at[:, :, 1], w2.at[:, :, :, c1:2 * c1]),
-                (k2.at[:, :, 2], w2.at[:, :, :, 2 * c1:3 * c1]),
-            ]
-        )
-    ]
+    moves = []
+    for j, slot in ((0, 0), (1, 1), (2, 3)):
+        for k, blocks in ((0, ((0, 1), (1, 2))), (1, ((0, 0), (1, 1))), (2, ((0, 3), (1, 0)))):
+            for a, b in blocks:
+                moves.append((k1.at[:, j, k], u1.at[slot, :, a * c0:(a + 1) * c0, b * c0:(b + 1) * c0]))
+    n_first = len(moves)
+    moves.append((kd.at[:, 1], wd.at[:, 0:c0, 0:c1]))
+    moves.append((kd.at[:, 2], wd.at[:, c0:2 * c0, 0:c1]))
+    moves.append((kd.at[:, 0], wd.at[:, c0:2 * c0, c1:2 * c1]))
+    n_down = len(moves)
+    for j, slot in ((0, 0), (1, 1), (2, 3)):
+        for k in range(3):
+            moves.append((k2.at[:, j, k], u2.at[slot, :, :, k * c1:(k + 1) * c1]))
+    weights = [pltpu.make_async_copy(src, dst, wsem.at[n]) for n, (src, dst) in enumerate(moves)]
     for copy in weights:
         copy.start()
 
@@ -152,8 +154,9 @@
         hx[:, rows + 1] = jnp.zeros((2, cols, c0), BF)
         mid[0:2, half + 1] = jnp.zeros((2, pairs, c1), BF)
 
-    w1[:, :, 0:c0, 2 * c0:3 * c0] = jnp.zeros((3, 3, c0, c0), BF)
-    w1[:, :, c0:2 * c0, 3 * c0:4 * c0] = jnp.zeros((3, 3, c0, c0), BF)
+    for slot in (0, 1, 3):
+        u1[slot, :, 0:c0, 2 * c0:3 * c0] = jnp.zeros((3, c0, c0), BF)
+        u1[slot, :, c0:2 * c0, 3 * c0:4 * c0] = jnp.zeros((3, c0, c0), BF)
     wd[:, 0:c0, c1:2 * c1] = jnp.zeros((3, c0, c1), BF)
 
     def paired(value):
@@ -178,31 +181,54 @@
     for side, row in ((0, 0), (1, rows + 1)):
         act[2:, row] = silu(paired(hr[side])).astype(BF)
 
-    for copy in weights[:6]:
-        copy.wait()
-
-    block = 8
-
-    def conv_first(f):
+    def taps(u):
+        step = 32
+        per = u.shape[2] // step
+
         def body(n, carry):
-            r = n * block
+            i, r = n // per, pl.multiple_of((n % per) * step, step)
+            g0, g1, g2 = (0.5 * u[m, i, pl.ds(r, step)].astype(F32) for m in (0, 1, 3))
+            u[1, i, pl.ds(r, step)] = (g0 + g2 + g1).astype(BF)
+            u[2, i, pl.ds(r, step)] = (g0 + g2 - g1).astype(BF)
+            return carry
+
+        lax.fori_loop(0, 3 * per, body, 0)
+
+    def transform(src, dst, g):
+        def body(n, carry):
+            cells = products(*[src[g, 2 * n + j] for j in range(4)])
+            for m in range(4):
+                dst[g, m, n] = cells[m]
+            return carry
+
+        lax.fori_loop(0, dst.shape[2], body, 0)
+
+    def filtered(v, u, group):
+        width = v.shape[-1]
+        size = v.shape[2] * pairs
+        n_out = u.shape[-1]
+        held = sums.at[:, :, 0:n_out]
+        for m in range(4):
             left = jnp.concatenate(
                 [
-                    act[f + i, pl.ds(r + j, block)].reshape(block * pairs, 2 * c0)
-                    for i in range(3) for j in range(3)
+                    jnp.concatenate([v[f + i, m].reshape(size, width) for i in range(3)], axis=1)
+                    for f in group
                 ],
-                axis=1,
+                axis=0,
             )
-            total = jnp.dot(left, w1[...].reshape(9 * 2 * c0, 4 * c0), preferred_element_type=F32)
-            bias = b1[...]
-            base = feat[f, pl.ds(r, block)].reshape(block * pairs, 2 * c0).astype(F32)
+            right = u[m].reshape(3 * width, u.shape[-1])
+            held[m] = jnp.dot(left, right, preferred_element_type=F32)
+        return held[0] + held[1] + held[2], held[1] - held[2] - held[3]
+
+    def conv_first(f):
+        bias = b1[...]
+        for parity, total in enumerate(filtered(v1, u1, [f])):
+            base = jnp.concatenate([feat[f, 2 * n + parity] for n in range(half)], axis=0).astype(F32)
             even = base[:, :c0] + bias + total[:, :c0] + before(total[:, 2 * c0:3 * c0], pairs)
             odd = base[:, c0:] + bias + total[:, c0:2 * c0] + after(total[:, 3 * c0:], pairs)
-            both = jnp.concatenate([even, odd], axis=1).astype(BF)
-            fo[f, pl.ds(r + 1, block)] = both.reshape(block, pairs, 2 * c0)
-            return carry
-
-        lax.fori_loop(0, rows // block, body, 0)
+            both = jnp.concatenate([even, odd], axis=1).astype(BF).reshape(half, pairs, 2 * c0)
+            for n in range(half):
+                fo[f, 2 * n + parity + 1] = both[n]
         start(f"fo{f}")
 
     def downsample(f):
@@ -222,19 +248,20 @@
             start(f"mt{f}", f"ma{f}", f"mb{f}")
         start(f"mu{f}", f"md{f}")
 
-    def conv_second(f):
-        left = jnp.concatenate(
-            [
-                mid[f + i, j:j + half].reshape(half * pairs, c1)
-                for i in range(3) for j in range(3)
-            ],
-            axis=1,
-        )
-        total = jnp.dot(left, w2[...].reshape(9 * c1, 3 * c1), preferred_element_type=F32)
-        value = red[f].reshape(half * pairs, c1).astype(F32) + b2[...]
-        value = value + total[:, c1:2 * c1] + before(total[:, :c1], pairs) + after(total[:, 2 * c1:], pairs)
-        res[f] = value.astype(BF).reshape(half, pairs, c1)
-        pltpu.make_async_copy(res.at[f], out.at[f], osem.at[f]).start()
+    def conv_second(group):
+        quarter = half // 2
+        for parity, total in enumerate(filtered(v2, u2, group)):
+            base = jnp.concatenate(
+                [red[f, 2 * n + parity] for f in group for n in range(quarter)], axis=0
+            ).astype(F32)
+            value = base + b2[...] + total[:, c1:2 * c1]
+            value = value + before(total[:, :c1], pairs) + after(total[:, 2 * c1:], pairs)
+            value = value.astype(BF).reshape(len(group) * quarter, pairs, c1)
+            for g, f in enumerate(group):
+                for n in range(quarter):
+                    res[f, 2 * n + parity] = value[g * quarter + n]
+        for f in group:
+            pltpu.make_async_copy(res.at[f], out.at[f], osem.at[f]).start()
 
     def halo(g):
         def body(n, carry):
@@ -242,31 +269,39 @@
             return carry
 
         lax.fori_loop(0, (rows + 2) // 3, body, 0)
-
-    conv_first(3)
-    conv_first(2)
-    for copy in weights[6:9]:
+        transform(act, v1, g)
+
+    for copy in weights[:n_first]:
         copy.wait()
-    downsample(3)
+    taps(u1)
+    for g in range(2, frames + 2):
+        transform(act, v1, g)
+
+    conv_first(last)
+    conv_first(prev)
+    for copy in weights[n_first:n_down]:
+        copy.wait()
+    downsample(last)
+    for copy in weights[n_down:]:
+        copy.wait()
+    taps(u2)
     arrived("t1", "tu", "td")
     halo(1)
     conv_first(1)
-    downsample(2)
+    downsample(prev)
     arrived("t0")
     halo(0)
     conv_first(0)
     downsample(1)
     downsample(0)
-    for copy in weights[9:]:
-        copy.wait()
-    for f in range(frames):
+    for f in reversed(range(frames)):
         arrived(f"mu{f}", f"md{f}")
-    conv_second(3)
-    conv_second(2)
-    arrived("mt3", "ma3", "mb3")
-    conv_second(1)
-    arrived("mt2", "ma2", "mb2")
-    conv_second(0)
+        transform(mid, v2, f + 2)
+    conv_second([last, prev])
+    for f in (last, prev):
+        arrived(f"mt{f}", f"ma{f}", f"mb{f}")
+        transform(mid, v2, f - prev)
+    conv_second([1, 0])
 
     for name in plan:
         @pl.when(there(*plan[name][3:]))
@@ -294,16 +329,19 @@
             pltpu.VMEM((4 * cols, c0), F32),
             pltpu.VMEM((frames + 2, rows + 2, pairs, 2 * c0), BF),
             pltpu.VMEM((frames, rows, pairs, 2 * c0), BF),
-            pltpu.VMEM((3, 3, 2 * c0, 4 * c0), BF),
+            pltpu.VMEM((frames + 2, 4, half, pairs, 2 * c0), BF),
+            pltpu.VMEM((4, 3, 2 * c0, 4 * c0), BF),
             pltpu.VMEM((3, 2 * c0, 2 * c1), BF),
-            pltpu.VMEM((3, 3, c1, 3 * c1), BF),
+            pltpu.VMEM((frames + 2, 4, half // 2, pairs, c1), BF),
+            pltpu.VMEM((4, 3, c1, 3 * c1), BF),
             pltpu.VMEM((frames, rows + 1, pairs, 2 * c0), BF),
             pltpu.VMEM((frames, half, pairs, c1), BF),
             pltpu.VMEM((frames + 2, half + 2, pairs, c1), BF),
             pltpu.VMEM((frames, half, pairs, c1), BF),
+            pltpu.VMEM((4, half * pairs, 3 * c1), F32),
             pltpu.SemaphoreType.DMA((copies,)),
             pltpu.SemaphoreType.DMA((copies,)),
-            pltpu.SemaphoreType.DMA((12,)),
+            pltpu.SemaphoreType.DMA((30,)),
             pltpu.SemaphoreType.DMA((frames,)),
         ],
         compiler_params=pltpu.CompilerParams(

time: 44.4 us -> 41.1 us (0.926)
  Pallas kernels: 41.8 us -> 38.6 us
    pallas_call x1, Pallas kernels: 41.8 us -> 38.6 us  [on_device(): pl.pallas_call(functools.partial(kernel, nt, ns), out_shape=jax.ShapeDtyp...]
where the time goes in v1:
time: 41.1 us; the launch traced here: 40.9 us
  Pallas kernels  38.6 us (94%)
  local copies, waits for them, and re-layouts  2.3 us (6%)
    pallas_call x1, Pallas kernels, on_device(): pl.pallas_call(functools.partial(kernel, nt, ns), out_shape=jax.ShapeDtyp...  38.6 us
    unnamed x1, local copies, waits for them, and re-layouts  2.3 us

profile of v1, /device:TPU:20, one launch (start us, length us, event | category | flops | bytes accessed | tf_op | source)
XLA Modules:
  0.0 40.9 jit_solution(14848723306434638481)
XLA Ops:
  0.0 38.6 %shard_map.73 = bf16[4,8,64,256]{3,2,1,0:T(8,128)(2,1)} custom-call(bf16[4,16,128,128]{3,2,1,0:T(8,128)(2,1)} %x.1, f32[1,128]{1,0:T(1,128)} %bitcast.5, f32[1,256]{1,0:T(1,128)} %bitcast.3, f32[1,256]{1,0:T(1,128)} %bitcast.4, bf16[3,3,3,128,128]{4,3,2,1,0:T(8,128)(2,1)} %k1.1, bf16[3,3,128,256]{3,2,1,0:T(8,128)(2,1)} %kd.1, bf16[3,3,3,256,256]{4,3,2,1,0:T(8,128)(2,1)} %k2.1), custom_call_target="tpu_custom_call" | custom-call | flops 16000000000 | bytes 10000000 | tf_op jit(solution)/shard_map/pallas_call | solution.py:321
  38.6 2.3 %copy.9 = bf16[4,8,64,256]{3,2,1,0:T(8,128)(2,1)} copy(bf16[4,8,64,256]{3,2,1,0:T(8,128)(2,1)} %shard_map.73) | data formatting | bytes 2097152

commit v2 on v1

--- a/solution.py
+++ b/solution.py
@@ -36,8 +36,8 @@
 
 def kernel(
     nt, ns, x, b1, bd, b2, k1, kd, k2, out,
-    hx, hr, lines, act, feat, v1, u1, wd, v2, u2, fo, red, mid, res, sums,
-    send, recv, wsem, osem,
+    raw, lines, act, feat, v1, u1, wd, v2, u2, fo, red, mid, res, sums,
+    send, recv, wsem, osem, xsem,
 ):
     t, s = lax.axis_index("tm"), lax.axis_index("space")
     frames, rows, cols, c0 = x.shape
@@ -71,6 +71,9 @@
     for j, slot in ((0, 0), (1, 1), (2, 3)):
         for k in range(3):
             moves.append((k2.at[:, j, k], u2.at[slot, :, :, k * c1:(k + 1) * c1]))
+    loads = [pltpu.make_async_copy(x.at[f], raw.at[f], xsem.at[f]) for f in range(frames)]
+    for copy in reversed(loads):
+        copy.start()
     weights = [pltpu.make_async_copy(src, dst, wsem.at[n]) for n, (src, dst) in enumerate(moves)]
     for copy in weights:
         copy.start()
@@ -82,7 +85,6 @@
             pl.semaphore_signal(barrier, inc=1, device_id=place(dt, ds), device_id_type=MESH)
     near_t = jnp.where(t > 0, 1, 0) + jnp.where(t < nt - 1, 1, 0) + 1
     near_s = jnp.where(s > 0, 1, 0) + jnp.where(s < ns - 1, 1, 0) + 1
-    pl.semaphore_wait(barrier, near_t * near_s - 1)
 
     plan = {}
 
@@ -90,21 +92,16 @@
         plan[name] = (src, dst, len(plan), dt, ds)
 
     last, prev = frames - 1, frames - 2
-    add("up", x.at[:, 0], hr.at[1], 0, -1)
-    add("down", x.at[:, rows - 1], hr.at[0], 0, 1)
-    add("t1", x.at[last], hx.at[1, 1:rows + 1], 1, 0)
-    add("tu", x.at[prev:frames, 0], hx.at[:, rows + 1], 1, -1)
-    add("td", x.at[prev:frames, rows - 1], hx.at[:, 0], 1, 1)
-    add("t0", x.at[prev], hx.at[0, 1:rows + 1], 1, 0)
     for f in range(frames):
         add(f"fo{f}", fo.at[f, rows], fo.at[f, 0], 0, 1)
-        add(f"mu{f}", mid.at[f + 2, 1], mid.at[f + 2, half + 1], 0, -1)
-        add(f"md{f}", mid.at[f + 2, half], mid.at[f + 2, 0], 0, 1)
-        if f >= prev:
-            g = f - prev
-            add(f"mt{f}", mid.at[f + 2, 1:half + 1], mid.at[g, 1:half + 1], 1, 0)
-            add(f"ma{f}", mid.at[f + 2, 1], mid.at[g, half + 1], 1, -1)
-            add(f"mb{f}", mid.at[f + 2, half], mid.at[g, 0], 1, 1)
+        for kind, ref, end in (("a", act, rows), ("m", mid, half)):
+            add(f"{kind}u{f}", ref.at[f + 2, 1], ref.at[f + 2, end + 1], 0, -1)
+            add(f"{kind}d{f}", ref.at[f + 2, end], ref.at[f + 2, 0], 0, 1)
+            if f >= prev:
+                g = f - prev
+                add(f"{kind}t{f}", ref.at[f + 2, 1:end + 1], ref.at[g, 1:end + 1], 1, 0)
+                add(f"{kind}x{f}", ref.at[f + 2, 1], ref.at[g, end + 1], 1, -1)
+                add(f"{kind}y{f}", ref.at[f + 2, end], ref.at[g, 0], 1, 1)
 
     def remote(name):
         src, dst, n, dt, ds = plan[name]
@@ -126,88 +123,81 @@
             def _():
                 remote(name).wait_recv()
 
-    start("up", "down", "t1", "tu", "td", "t0")
-
-    @pl.when(t == 0)
-    def _():
-        hx[...] = jnp.zeros_like(hx)
-        mid[0:2] = jnp.zeros((2,) + mid.shape[1:], BF)
+    def send_frame(kind, f):
+        if f >= prev:
+            start(f"{kind}t{f}", f"{kind}x{f}", f"{kind}y{f}")
+        start(f"{kind}u{f}", f"{kind}d{f}")
+
+    def borders(kind, f):
+        arrived(f"{kind}u{f}", f"{kind}d{f}")
+
+    def earlier(kind, f):
+        arrived(f"{kind}t{f}", f"{kind}x{f}", f"{kind}y{f}")
+
+    for ref, end in ((act, rows), (mid, half)):
+        line = ref.shape[2:]
+
+        @pl.when(t == 0)
+        def _():
+            ref[0:2] = jnp.zeros((2,) + ref.shape[1:], BF)
+
+        for here, row in ((s == 0, 0), (s == ns - 1, end + 1)):
+            @pl.when(here)
+            def _():
+                ref[2:, row] = jnp.zeros((frames,) + line, BF)
+
+            @pl.when(jnp.logical_and(t > 0, here))
+            def _():
+                ref[0:2, row] = jnp.zeros((2,) + line, BF)
 
     @pl.when(s == 0)
     def _():
-        hr[0] = jnp.zeros(hr.shape[1:], BF)
         fo[:, 0] = jnp.zeros((frames, pairs, 2 * c0), BF)
-        mid[2:, 0] = jnp.zeros((frames, pairs, c1), BF)
-
-    @pl.when(s == ns - 1)
-    def _():
-        hr[1] = jnp.zeros(hr.shape[1:], BF)
-        mid[2:, half + 1] = jnp.zeros((frames, pairs, c1), BF)
-
-    @pl.when(jnp.logical_and(t > 0, s == 0))
-    def _():
-        hx[:, 0] = jnp.zeros((2, cols, c0), BF)
-        mid[0:2, 0] = jnp.zeros((2, pairs, c1), BF)
-
-    @pl.when(jnp.logical_and(t > 0, s == ns - 1))
-    def _():
-        hx[:, rows + 1] = jnp.zeros((2, cols, c0), BF)
-        mid[0:2, half + 1] = jnp.zeros((2, pairs, c1), BF)
 
     for slot in (0, 1, 3):
         u1[slot, :, 0:c0, 2 * c0:3 * c0] = jnp.zeros((3, c0, c0), BF)
         u1[slot, :, c0:2 * c0, 3 * c0:4 * c0] = jnp.zeros((3, c0, c0), BF)
     wd[:, 0:c0, c1:2 * c1] = jnp.zeros((3, c0, c1), BF)
 
-    def paired(value):
-        count = value.shape[0]
-        lines[0:count * cols] = value.reshape(count * cols, c0).astype(F32)
-        even = lines[pl.ds(0, count * pairs, stride=2), :]
-        odd = lines[pl.ds(1, count * pairs, stride=2), :]
-        both = jnp.concatenate([even, odd], axis=1)
-        return both.reshape(count, pairs, 2 * c0)
-
     step = 4
 
-    def own(n, carry):
-        f, r = n // (rows // step), (n % (rows // step)) * step
-        both = paired(x[f, pl.ds(r, step)])
+    def prepare(f, r, slot):
+        count = step * cols
+        base = slot * count
+        lines[base:base + count] = raw[f, pl.ds(r, step)].reshape(count, c0).astype(F32)
+        even = lines[pl.ds(base, count // 2, stride=2), :]
+        odd = lines[pl.ds(base + 1, count // 2, stride=2), :]
+        both = jnp.concatenate([even, odd], axis=1).reshape(step, pairs, 2 * c0)
         feat[f, pl.ds(r, step)] = both.astype(BF)
         act[f + 2, pl.ds(r + 1, step)] = silu(both).astype(BF)
-        return carry
-
-    lax.fori_loop(0, frames * rows // step, own, 0)
-    arrived("up", "down")
-    for side, row in ((0, 0), (1, rows + 1)):
-        act[2:, row] = silu(paired(hr[side])).astype(BF)
-
-    def taps(u):
-        step = 32
-        per = u.shape[2] // step
-
+
+    def own(f):
         def body(n, carry):
-            i, r = n // per, pl.multiple_of((n % per) * step, step)
-            g0, g1, g2 = (0.5 * u[m, i, pl.ds(r, step)].astype(F32) for m in (0, 1, 3))
-            u[1, i, pl.ds(r, step)] = (g0 + g2 + g1).astype(BF)
-            u[2, i, pl.ds(r, step)] = (g0 + g2 - g1).astype(BF)
+            for slot in range(2):
+                prepare(f, (2 * n + slot) * step, slot)
             return carry
 
-        lax.fori_loop(0, 3 * per, body, 0)
+        lax.fori_loop(0, rows // (2 * step), body, 0)
+
+    def taps(u, i):
+        size = 32
+        for r in range(0, u.shape[2], size):
+            outer = u[0, i, r:r + size] + u[3, i, r:r + size]
+            inner = u[1, i, r:r + size]
+            u[1, i, r:r + size] = (outer + inner) * 0.5
+            u[2, i, r:r + size] = (outer - inner) * 0.5
 
     def transform(src, dst, g):
-        def body(n, carry):
+        for n in range(dst.shape[2]):
             cells = products(*[src[g, 2 * n + j] for j in range(4)])
             for m in range(4):
                 dst[g, m, n] = cells[m]
-            return carry
-
-        lax.fori_loop(0, dst.shape[2], body, 0)
-
-    def filtered(v, u, group):
+
+    def filtered(v, u, group, beside=None):
         width = v.shape[-1]
         size = v.shape[2] * pairs
         n_out = u.shape[-1]
-        held = sums.at[:, :, 0:n_out]
+        held = sums.at[:, 0:len(group) * size, 0:n_out]
         for m in range(4):
             left = jnp.concatenate(
                 [
@@ -218,11 +208,13 @@
             )
             right = u[m].reshape(3 * width, u.shape[-1])
             held[m] = jnp.dot(left, right, preferred_element_type=F32)
+            if beside:
+                beside(m)
         return held[0] + held[1] + held[2], held[1] - held[2] - held[3]
 
-    def conv_first(f):
+    def conv_first(f, beside=None):
         bias = b1[...]
-        for parity, total in enumerate(filtered(v1, u1, [f])):
+        for parity, total in enumerate(filtered(v1, u1, [f], beside)):
             base = jnp.concatenate([feat[f, 2 * n + parity] for n in range(half)], axis=0).astype(F32)
             even = base[:, :c0] + bias + total[:, :c0] + before(total[:, 2 * c0:3 * c0], pairs)
             odd = base[:, c0:] + bias + total[:, c0:2 * c0] + after(total[:, 3 * c0:], pairs)
@@ -244,9 +236,7 @@
         value = (total[:, :c1] + before(total[:, c1:], pairs) + bd[...]).astype(BF)
         red[f] = value.reshape(half, pairs, c1)
         mid[f + 2, 1:half + 1] = silu(value.astype(F32)).astype(BF).reshape(half, pairs, c1)
-        if f >= prev:
-            start(f"mt{f}", f"ma{f}", f"mb{f}")
-        start(f"mu{f}", f"md{f}")
+        send_frame("m", f)
 
     def conv_second(group):
         quarter = half // 2
@@ -263,45 +253,57 @@
         for f in group:
             pltpu.make_async_copy(res.at[f], out.at[f], osem.at[f]).start()
 
-    def halo(g):
-        def body(n, carry):
-            act[g, pl.ds(n * 3, 3)] = silu(paired(hx[g, pl.ds(n * 3, 3)])).astype(BF)
-            return carry
-
-        lax.fori_loop(0, (rows + 2) // 3, body, 0)
-        transform(act, v1, g)
-
+    def prepare_first(m):
+        for n in range(m, rows // step, 4):
+            prepare(0, n * step, 0)
+
+    def second_taps(m):
+        if m < 3:
+            taps(u2, m)
+
+    for f in range(last, 0, -1):
+        loads[f].wait()
+        own(f)
+        if f == last:
+            pl.semaphore_wait(barrier, near_t * near_s - 1)
+        send_frame("a", f)
+    loads[0].wait()
     for copy in weights[:n_first]:
         copy.wait()
-    taps(u1)
-    for g in range(2, frames + 2):
-        transform(act, v1, g)
-
-    conv_first(last)
-    conv_first(prev)
-    for copy in weights[n_first:n_down]:
+    for i in range(3):
+        taps(u1, i)
+    for f in range(last, 0, -1):
+        borders("a", f)
+        transform(act, v1, f + 2)
+    conv_first(last, prepare_first)
+    send_frame("a", 0)
+    for copy in weights[n_first:]:
         copy.wait()
+    borders("a", 0)
+    transform(act, v1, 2)
+    conv_first(prev, second_taps)
     downsample(last)
-    for copy in weights[n_down:]:
-        copy.wait()
-    taps(u2)
-    arrived("t1", "tu", "td")
-    halo(1)
+    earlier("a", last)
+    transform(act, v1, 1)
     conv_first(1)
     downsample(prev)
-    arrived("t0")
-    halo(0)
+    earlier("a", prev)
+    transform(act, v1, 0)
     conv_first(0)
     downsample(1)
+    for f in (last, prev):
+        borders("m", f)
+        transform(mid, v2, f + 2)
     downsample(0)
-    for f in reversed(range(frames)):
-        arrived(f"mu{f}", f"md{f}")
-        transform(mid, v2, f + 2)
-    conv_second([last, prev])
+    borders("m", 1)
+    transform(mid, v2, 3)
+    conv_second([last])
+    borders("m", 0)
     for f in (last, prev):
-        arrived(f"mt{f}", f"ma{f}", f"mb{f}")
-        transform(mid, v2, f - prev)
-    conv_second([1, 0])
+        earlier("m", f)
+    for g in range(3):
+        transform(mid, v2, g)
+    conv_second(list(range(prev, -1, -1)))
 
     for name in plan:
         @pl.when(there(*plan[name][3:]))
@@ -317,16 +319,15 @@
     half, pairs = rows // 2, cols // 2
     vmem = pl.BlockSpec(memory_space=pltpu.VMEM)
     hbm = pl.BlockSpec(memory_space=pl.ANY)
-    copies = 6 + 3 * frames + 6
+    copies = 5 * frames + 12
     return pl.pallas_call(
         functools.partial(kernel, nt, ns),
         out_shape=jax.ShapeDtypeStruct((frames, half, pairs, c1), BF),
-        in_specs=[vmem] * 4 + [hbm] * 3,
+        in_specs=[hbm] + [vmem] * 3 + [hbm] * 3,
         out_specs=hbm,
         scratch_shapes=[
-            pltpu.VMEM((2, rows + 2, cols, c0), BF),
-            pltpu.VMEM((2, frames, cols, c0), BF),
-            pltpu.VMEM((4 * cols, c0), F32),
+            pltpu.VMEM((frames, rows, cols, c0), BF),
+            pltpu.VMEM((8 * cols, c0), F32),
             pltpu.VMEM((frames + 2, rows + 2, pairs, 2 * c0), BF),
             pltpu.VMEM((frames, rows, pairs, 2 * c0), BF),
             pltpu.VMEM((frames + 2, 4, half, pairs, 2 * c0), BF),
@@ -338,10 +339,11 @@
             pltpu.VMEM((frames, half, pairs, c1), BF),
             pltpu.VMEM((frames + 2, half + 2, pairs, c1), BF),
             pltpu.VMEM((frames, half, pairs, c1), BF),
-            pltpu.VMEM((4, half * pairs, 3 * c1), F32),
+            pltpu.VMEM((4, max(half, 3 * half // 2) * pairs, 3 * c1), F32),
             pltpu.SemaphoreType.DMA((copies,)),
             pltpu.SemaphoreType.DMA((copies,)),
             pltpu.SemaphoreType.DMA((30,)),
+            pltpu.SemaphoreType.DMA((frames,)),
             pltpu.SemaphoreType.DMA((frames,)),
         ],
         compiler_params=pltpu.CompilerParams(

time: 41.1 us -> 42.3 us (1.029)
  the two profiles are of different devices: /device:TPU:20 before, /device:TPU:18 now
where the time goes in v2:
time: 42.3 us; the launch traced here: 42.2 us
  Pallas kernels  39.9 us (94%)
  local copies, waits for them, and re-layouts  2.3 us (5%)
    pallas_call x1, Pallas kernels, on_device(): pl.pallas_call(functools.partial(kernel, nt, ns), out_shape=jax.ShapeDtyp...  39.9 us
    unnamed x1, local copies, waits for them, and re-layouts  2.3 us

profile of v2, /device:TPU:18, one launch (start us, length us, event | category | flops | bytes accessed | tf_op | source)
XLA Modules:
  0.0 42.2 jit_solution(17434738832451013237)
XLA Ops:
  0.0 39.9 %shard_map.73 = bf16[4,8,64,256]{3,2,1,0:T(8,128)(2,1)} custom-call(bf16[4,16,128,128]{3,2,1,0:T(8,128)(2,1)} %x.1, f32[1,128]{1,0:T(1,128)} %bitcast.5, f32[1,256]{1,0:T(1,128)} %bitcast.3, f32[1,256]{1,0:T(1,128)} %bitcast.4, bf16[3,3,3,128,128]{4,3,2,1,0:T(8,128)(2,1)} %k1.1, bf16[3,3,128,256]{3,2,1,0:T(8,128)(2,1)} %kd.1, bf16[3,3,3,256,256]{4,3,2,1,0:T(8,128)(2,1)} %k2.1), custom_call_target="tpu_custom_call" | custom-call | flops 16000000000 | bytes 10000000 | tf_op jit(solution)/shard_map/pallas_call | solution.py:323
  39.9 2.3 %copy.9 = bf16[4,8,64,256]{3,2,1,0:T(8,128)(2,1)} copy(bf16[4,8,64,256]{3,2,1,0:T(8,128)(2,1)} %shard_map.73) | data formatting | bytes 2097152

commit v3 on v2

--- a/solution.py
+++ b/solution.py
@@ -123,10 +123,12 @@
             def _():
                 remote(name).wait_recv()
 
-    def send_frame(kind, f):
+    def send_borders(kind, f):
+        start(f"{kind}u{f}", f"{kind}d{f}")
+
+    def send_later(kind, f):
         if f >= prev:
-            start(f"{kind}t{f}", f"{kind}x{f}", f"{kind}y{f}")
-        start(f"{kind}u{f}", f"{kind}d{f}")
+            start(f"{kind}x{f}", f"{kind}y{f}", f"{kind}t{f}")
 
     def borders(kind, f):
         arrived(f"{kind}u{f}", f"{kind}d{f}")
@@ -159,7 +161,7 @@
         u1[slot, :, c0:2 * c0, 3 * c0:4 * c0] = jnp.zeros((3, c0, c0), BF)
     wd[:, 0:c0, c1:2 * c1] = jnp.zeros((3, c0, c1), BF)
 
-    step = 4
+    step = 2
 
     def prepare(f, r, slot):
         count = step * cols
@@ -173,11 +175,11 @@
 
     def own(f):
         def body(n, carry):
-            for slot in range(2):
-                prepare(f, (2 * n + slot) * step, slot)
+            for slot in range(4):
+                prepare(f, (4 * n + slot) * step, slot)
             return carry
 
-        lax.fori_loop(0, rows // (2 * step), body, 0)
+        lax.fori_loop(0, rows // (4 * step), body, 0)
 
     def taps(u, i):
         size = 32
@@ -210,17 +212,23 @@
             held[m] = jnp.dot(left, right, preferred_element_type=F32)
             if beside:
                 beside(m)
-        return held[0] + held[1] + held[2], held[1] - held[2] - held[3]
+        return held
+
+    def combined(held, at, parity):
+        part = pl.ds(at, pairs)
+        one, two = held[1, part], held[2, part]
+        return held[0, part] + one + two if parity == 0 else one - two - held[3, part]
 
     def conv_first(f, beside=None):
         bias = b1[...]
-        for parity, total in enumerate(filtered(v1, u1, [f], beside)):
-            base = jnp.concatenate([feat[f, 2 * n + parity] for n in range(half)], axis=0).astype(F32)
-            even = base[:, :c0] + bias + total[:, :c0] + before(total[:, 2 * c0:3 * c0], pairs)
-            odd = base[:, c0:] + bias + total[:, c0:2 * c0] + after(total[:, 3 * c0:], pairs)
-            both = jnp.concatenate([even, odd], axis=1).astype(BF).reshape(half, pairs, 2 * c0)
-            for n in range(half):
-                fo[f, 2 * n + parity + 1] = both[n]
+        held = filtered(v1, u1, [f], beside)
+        for n in range(half):
+            for parity in range(2):
+                total = combined(held, n * pairs, parity)
+                base = feat[f, 2 * n + parity].astype(F32)
+                even = base[:, :c0] + bias + total[:, :c0] + before(total[:, 2 * c0:3 * c0], pairs)
+                odd = base[:, c0:] + bias + total[:, c0:2 * c0] + after(total[:, 3 * c0:], pairs)
+                fo[f, 2 * n + parity + 1] = jnp.concatenate([even, odd], axis=1).astype(BF)
         start(f"fo{f}")
 
     def downsample(f):
@@ -232,30 +240,33 @@
             ],
             axis=1,
         )
-        total = jnp.dot(left, wd[...].reshape(3 * 2 * c0, 2 * c1), preferred_element_type=F32)
-        value = (total[:, :c1] + before(total[:, c1:], pairs) + bd[...]).astype(BF)
-        red[f] = value.reshape(half, pairs, c1)
-        mid[f + 2, 1:half + 1] = silu(value.astype(F32)).astype(BF).reshape(half, pairs, c1)
-        send_frame("m", f)
+        held = sums.at[0, 0:half * pairs, 0:2 * c1]
+        held[...] = jnp.dot(left, wd[...].reshape(3 * 2 * c0, 2 * c1), preferred_element_type=F32)
+        for n in range(half):
+            total = held[n * pairs:(n + 1) * pairs]
+            value = (total[:, :c1] + before(total[:, c1:], pairs) + bd[...]).astype(BF)
+            red[f, n] = value
+            mid[f + 2, n + 1] = silu(value.astype(F32)).astype(BF)
+        send_borders("m", f)
+        send_later("m", f)
 
     def conv_second(group):
         quarter = half // 2
-        for parity, total in enumerate(filtered(v2, u2, group)):
-            base = jnp.concatenate(
-                [red[f, 2 * n + parity] for f in group for n in range(quarter)], axis=0
-            ).astype(F32)
-            value = base + b2[...] + total[:, c1:2 * c1]
-            value = value + before(total[:, :c1], pairs) + after(total[:, 2 * c1:], pairs)
-            value = value.astype(BF).reshape(len(group) * quarter, pairs, c1)
-            for g, f in enumerate(group):
-                for n in range(quarter):
-                    res[f, 2 * n + parity] = value[g * quarter + n]
-        for f in group:
+        held = filtered(v2, u2, group)
+        for g, f in enumerate(group):
+            for n in range(quarter):
+                for parity in range(2):
+                    total = combined(held, (g * quarter + n) * pairs, parity)
+                    value = red[f, 2 * n + parity].astype(F32) + b2[...] + total[:, c1:2 * c1]
+                    value = value + before(total[:, :c1], pairs) + after(total[:, 2 * c1:], pairs)
+                    res[f, 2 * n + parity] = value.astype(BF)
             pltpu.make_async_copy(res.at[f], out.at[f], osem.at[f]).start()
 
+    inner = list(range(step, rows - step, step))
+
     def prepare_first(m):
-        for n in range(m, rows // step, 4):
-            prepare(0, n * step, 0)
+        for n in inner[m::4]:
+            prepare(0, n, m)
 
     def second_taps(m):
         if m < 3:
@@ -266,8 +277,12 @@
         own(f)
         if f == last:
             pl.semaphore_wait(barrier, near_t * near_s - 1)
-        send_frame("a", f)
+        send_borders("a", f)
     loads[0].wait()
+    prepare(0, 0, 0)
+    prepare(0, rows - step, 1)
+    send_borders("a", 0)
+    send_later("a", last)
     for copy in weights[:n_first]:
         copy.wait()
     for i in range(3):
@@ -276,7 +291,7 @@
         borders("a", f)
         transform(act, v1, f + 2)
     conv_first(last, prepare_first)
-    send_frame("a", 0)
+    send_later("a", prev)
     for copy in weights[n_first:]:
         copy.wait()
     borders("a", 0)

time: 42.3 us -> 37.9 us (0.90)
  the two profiles are of different devices: /device:TPU:18 before, /device:TPU:20 now
where the time goes in v3:
time: 37.9 us; the launch traced here: 37.7 us
  Pallas kernels  35.4 us (93%)
  local copies, waits for them, and re-layouts  2.3 us (6%)
    pallas_call x1, Pallas kernels, on_device(): pl.pallas_call(functools.partial(kernel, nt, ns), out_shape=jax.ShapeDtyp...  35.4 us
    unnamed x1, local copies, waits for them, and re-layouts  2.3 us

profile of v3, /device:TPU:20, one launch (start us, length us, event | category | flops | bytes accessed | tf_op | source)
XLA Modules:
  0.0 37.7 jit_solution(9935964772649404341)
XLA Ops:
  0.0 35.4 %shard_map.73 = bf16[4,8,64,256]{3,2,1,0:T(8,128)(2,1)} custom-call(bf16[4,16,128,128]{3,2,1,0:T(8,128)(2,1)} %x.1, f32[1,128]{1,0:T(1,128)} %bitcast.5, f32[1,256]{1,0:T(1,128)} %bitcast.3, f32[1,256]{1,0:T(1,128)} %bitcast.4, bf16[3,3,3,128,128]{4,3,2,1,0:T(8,128)(2,1)} %k1.1, bf16[3,3,128,256]{3,2,1,0:T(8,128)(2,1)} %kd.1, bf16[3,3,3,256,256]{4,3,2,1,0:T(8,128)(2,1)} %k2.1), custom_call_target="tpu_custom_call" | custom-call | flops 16000000000 | bytes 10000000 | tf_op jit(solution)/shard_map/pallas_call | solution.py:338
  35.4 2.3 %copy.9 = bf16[4,8,64,256]{3,2,1,0:T(8,128)(2,1)} copy(bf16[4,8,64,256]{3,2,1,0:T(8,128)(2,1)} %shard_map.73) | data formatting | bytes 2097152

commit v4 on v3

--- a/solution.py
+++ b/solution.py
@@ -175,11 +175,11 @@
 
     def own(f):
         def body(n, carry):
-            for slot in range(4):
-                prepare(f, (4 * n + slot) * step, slot)
+            for slot in range(2):
+                prepare(f, (2 * n + slot + 1) * step, slot)
             return carry
 
-        lax.fori_loop(0, rows // (4 * step), body, 0)
+        lax.fori_loop(0, (rows // step - 2) // 2, body, 0)
 
     def taps(u, i):
         size = 32
@@ -272,17 +272,17 @@
         if m < 3:
             taps(u2, m)
 
-    for f in range(last, 0, -1):
+    for f in range(last, -1, -1):
         loads[f].wait()
-        own(f)
+        prepare(f, 0, 0)
+        prepare(f, rows - step, 1)
         if f == last:
             pl.semaphore_wait(barrier, near_t * near_s - 1)
         send_borders("a", f)
-    loads[0].wait()
-    prepare(0, 0, 0)
-    prepare(0, rows - step, 1)
-    send_borders("a", 0)
-    send_later("a", last)
+    for f in range(last, 0, -1):
+        own(f)
+        if f == last:
+            send_later("a", f)
     for copy in weights[:n_first]:
         copy.wait()
     for i in range(3):
@@ -314,11 +314,12 @@
     transform(mid, v2, 3)
     conv_second([last])
     borders("m", 0)
+    transform(mid, v2, 2)
+    conv_second([prev])
     for f in (last, prev):
         earlier("m", f)
-    for g in range(3):
-        transform(mid, v2, g)
-    conv_second(list(range(prev, -1, -1)))
+        transform(mid, v2, f - prev)
+    conv_second([1, 0])
 
     for name in plan:
         @pl.when(there(*plan[name][3:]))

time: 37.9 us -> 38.1 us (level)
  no operation moved by 1% of the time
where the time goes in v4:
time: 38.1 us; the launch traced here: 38 us
  Pallas kernels  35.6 us (93%)
  local copies, waits for them, and re-layouts  2.3 us (6%)
    pallas_call x1, Pallas kernels, on_device(): pl.pallas_call(functools.partial(kernel, nt, ns), out_shape=jax.ShapeDtyp...  35.6 us
    unnamed x1, local copies, waits for them, and re-layouts  2.3 us

profile of v4, /device:TPU:20, one launch (start us, length us, event | category | flops | bytes accessed | tf_op | source)
XLA Modules:
  0.0 38.0 jit_solution(5531997919093836938)
XLA Ops:
  0.0 35.6 %shard_map.73 = bf16[4,8,64,256]{3,2,1,0:T(8,128)(2,1)} custom-call(bf16[4,16,128,128]{3,2,1,0:T(8,128)(2,1)} %x.1, f32[1,128]{1,0:T(1,128)} %bitcast.5, f32[1,256]{1,0:T(1,128)} %bitcast.3, f32[1,256]{1,0:T(1,128)} %bitcast.4, bf16[3,3,3,128,128]{4,3,2,1,0:T(8,128)(2,1)} %k1.1, bf16[3,3,128,256]{3,2,1,0:T(8,128)(2,1)} %kd.1, bf16[3,3,3,256,256]{4,3,2,1,0:T(8,128)(2,1)} %k2.1), custom_call_target="tpu_custom_call" | custom-call | flops 16000000000 | bytes 10000000 | tf_op jit(solution)/shard_map/pallas_call | solution.py:339
  35.6 2.3 %copy.9 = bf16[4,8,64,256]{3,2,1,0:T(8,128)(2,1)} copy(bf16[4,8,64,256]{3,2,1,0:T(8,128)(2,1)} %shard_map.73) | data formatting | bytes 2097152
